TPU v7x, 32 devices: a whole 2x2x4 slice. The times are simulated.
32 devices in a mesh: prow: 8 (over z, x), pcol: 4 (over y, core).
Axes of the slice: x: 2, y: 2, z: 4, core: 2. Of those that a mesh axis runs over, the one named last changes fastest.
Arguments:
- right_hand_blocks: float32 [8, 4, 512, 256], P('prow'), may hold values from -6 to 6
- diag_inverse: bfloat16 [8, 4, 512, 512], P('prow'), as said below
- lower_blocks: bfloat16 [8, 4, 3, 5, 512, 512], P('prow', 'pcol'), may hold values from -0.0625 to 0.0625
- block_source: int32 [8, 4, 3, 5], P('prow', 'pcol'), may hold values from 0 to 1, as said below
- target_level_per_slot: int32 [8, 4, 3, 5], P('prow', 'pcol'), may hold values from 1 to 4, as said below
Outputs:
- solved: bfloat16 [8, 4, 512, 256], P('prow')
Inputs may be any that keep to these rules, and one draw needn't show every extreme that they name: `target_level_per_slot`: block (source k, target level t) appears at most once among the slots of one device and one source level l; every target level exceeds l; the filled slots come first, and there are min(5, 2 * (3 - l)) of them. `block_source`: an empty slot has source 0. `diag_inverse`: lower triangular, diagonal between 0.5 and 1.5.
All inputs are finite; a program needn't handle non-finite values.
Results may differ from a plain program's by a relative error of at most 0.0075.
Values may be sent and summed in bfloat16 or wider, within the bound.
A program may use at most 128 MiB of HBM per device.

v0:
```python
import jax
import jax.numpy as jnp
from jax import lax
from jax.sharding import PartitionSpec as P


def on_device(right_hand_blocks, diag_inverse, lower_blocks, block_source, target_level_per_slot):
    col_count = lax.axis_size("pcol")
    row_count = lax.axis_size("prow")
    per_col = row_count // col_count
    column = lax.axis_index("pcol")
    levels = right_hand_blocks.shape[1]
    block_width = right_hand_blocks.shape[2]
    rhs_cols = right_hand_blocks.shape[3]
    partial_value = jnp.zeros((levels, block_width, rhs_cols), jnp.float32)
    outputs = []
    for tree_level in range(levels):
        inverse = diag_inverse[0, tree_level]
        given_rhs = right_hand_blocks[0, tree_level]
        if tree_level == 0:
            solved = jnp.dot(
                inverse, given_rhs.astype(jnp.bfloat16), preferred_element_type=jnp.float32
            ).astype(jnp.bfloat16)
        else:
            summed = lax.psum(partial_value[tree_level], "pcol")
            solved = jnp.dot(
                inverse,
                (given_rhs - summed).astype(jnp.bfloat16),
                preferred_element_type=jnp.float32,
            ).astype(jnp.bfloat16)
        outputs.append(solved)
        if tree_level < levels - 1:
            gathered = lax.all_gather(solved, "prow", axis=0, tiled=True)
            gathered = gathered.reshape(per_col, col_count, block_width, rhs_cols)
            by_slot = lax.dynamic_index_in_dim(gathered, column, 1, keepdims=False)
            sources = block_source[0, 0, tree_level]
            targets = target_level_per_slot[0, 0, tree_level]
            picked = jnp.take(by_slot, sources, axis=0)
            block_products = jnp.einsum(
                "bij,bjr->bir",
                lower_blocks[0, 0, tree_level],
                picked,
                preferred_element_type=jnp.float32,
            )
            indicator_matrix = (
                targets[None, :] == jnp.arange(levels, dtype=jnp.int32)[:, None]
            ).astype(jnp.float32)
            partial_value = partial_value + jnp.einsum(
                "tk,kxz->txz", indicator_matrix, block_products, precision=lax.Precision.HIGHEST
            )
    return jnp.stack(outputs, axis=0)[None]


def solution(mesh):
    placed = (
        P("prow", None, None, None),
        P("prow", None, None, None),
        P("prow", "pcol", None, None, None, None),
        P("prow", "pcol", None, None),
        P("prow", "pcol", None, None),
    )
    return jax.shard_map(
        on_device,
        mesh=mesh,
        in_specs=placed,
        out_specs=P("prow", None, None, None),
        check_vma=False,
    )
```

profile of v0, /device:TPU:3, one launch (start us, length us, event | category | flops | bytes accessed | tf_op | source)
XLA Modules:
  0.0 320.3 jit_solution(16675195253927854351)
XLA Ops:
  6.5 2.2 convolution_convert_fusion.3
  10.2 47.8 %all-gather.4.cloned.1.call-done = bf16[4096,256]{1,0:T(8,128)(2,1)} async-done(((bf16[512,256]{1,0:T(8,128)(2,1)}), bf16[4096,256]{1,0:T(8,128)(2,1)}) %all-gather.4.cloned.1.call-update) | async-done | bytes 2097168 | tf_op jit(solution)/shard_map/all_gather | solution.py:33
  59.1 1.8 gather_fusion
  60.9 3.2 fusion.10
  64.0 3.5 %copy.9 = f32[5,256,512]{1,0,2:T(8,128)} copy(f32[5,256,512]{2,1,0:T(8,128)S(1)} %fusion.10) | data formatting | bytes 5242880 | tf_op jit(solution)/shard_map/bij,bjr->bir/dot_general | solution.py:39
  67.6 4.2 %fusion.4 = f32[4,512,256]{2,0,1:T(4,128)S(1)} fusion(f32[5,256,512]{1,0,2:T(8,128)} %copy.9, s32[5]{0:T(128)S(1)} %get-tuple-element.13), kind=kOutput, calls=%fused_computation.7 | convolution fusion | flops 31457300 | bytes 4718612 | tf_op jit(solution)/shard_map/tk,kxz->txz/dot_general | solution.py:48
  73.2 32.9 %all-reduce.4.cloned.1.call-done = f32[512,256]{1,0:T(8,128)} async-done(((f32[512,256]{1,0:T(8,128)}), f32[512,256]{1,0:T(8,128)}) %all-reduce.4.cloned.1.call-update) | async-done | bytes 524304 | tf_op jit(solution)/shard_map/psum | solution.py:25
  106.1 2.4 convolution_convert_fusion.2
  108.6 48.3 %all-gather.6.cloned.1.call-done = bf16[4096,256]{1,0:T(8,128)(2,1)} async-done(((bf16[512,256]{1,0:T(8,128)(2,1)}), bf16[4096,256]{1,0:T(8,128)(2,1)}) %all-gather.6.cloned.1.call-update) | async-done | bytes 2097168 | tf_op jit(solution)/shard_map/all_gather | solution.py:33
  158.0 1.8 gather_fusion.1
  159.7 4.7 %fusion.8 = f32[5,256,512]{2,1,0:T(8,128)} fusion(bf16[1,1,3,5,512,512]{5,4,3,2,1,0:T(8,128)(2,1)} %param.9, bf16[5,512,256]{2,1,0:T(8,128)(2,1)} %gather_fusion.1, pred[5]{0:T(512)(128)(4,1)S(1)} %get-tuple-element.17), kind=kOutput, calls=%fused_computation.11 | convolution fusion | flops 671744000 | bytes 6553605 | tf_op jit(solution)/shard_map/bij,bjr->bir/dot_general | solution.py:39
  164.4 5.0 %copy.11 = f32[5,256,512]{1,0,2:T(8,128)} copy(f32[5,256,512]{2,1,0:T(8,128)} %fusion.8) | data formatting | bytes 5242880 | tf_op jit(solution)/shard_map/bij,bjr->bir/dot_general | solution.py:39
  169.5 4.4 %fusion.15 = f32[4,512,256]{2,0,1:T(4,128)S(1)} fusion(f32[4,512,256]{2,0,1:T(4,128)S(1)} %fusion.4, f32[5,256,512]{1,0,2:T(8,128)} %copy.11, s32[5]{0:T(128)S(1)} %get-tuple-element.14), kind=kOutput, calls=%fused_computation.18 | convolution fusion | flops 31981588 | bytes 6815764 | tf_op jit(solution)/shard_map/tk,kxz->txz/dot_general | solution.py:48
  173.8 1.3 copy-done
  176.6 32.9 %all-reduce.6.cloned.1.call-done = f32[512,256]{1,0:T(8,128)} async-done(((f32[512,256]{1,0:T(8,128)}), f32[512,256]{1,0:T(8,128)}) %all-reduce.6.cloned.1.call-update) | async-done | bytes 524304 | tf_op jit(solution)/shard_map/psum | solution.py:25
  209.5 2.4 convolution_convert_fusion.1
  212.2 48.1 %all-gather.8.cloned.1.call-done = bf16[4096,256]{1,0:T(8,128)(2,1)} async-done(((bf16[512,256]{1,0:T(8,128)(2,1)}), bf16[4096,256]{1,0:T(8,128)(2,1)}) %all-gather.8.cloned.1.call-update) | async-done | bytes 2097168 | tf_op jit(solution)/shard_map/all_gather | solution.py:33
  261.3 1.8 gather_fusion.2
  263.1 3.2 fusion.6
  266.3 3.5 %copy.13 = f32[5,256,512]{1,0,2:T(8,128)} copy(f32[5,256,512]{2,1,0:T(8,128)S(1)} %fusion.6) | data formatting | bytes 5242880 | tf_op jit(solution)/shard_map/bij,bjr->bir/dot_general | solution.py:39
  269.8 4.2 %fusion = f32[4,512,256]{2,0,1:T(4,128)S(1)} fusion(f32[5,256,512]{1,0,2:T(8,128)} %copy.13, s32[5]{0:T(128)S(1)} %get-tuple-element.12), kind=kOutput, calls=%fused_computation.3 | convolution fusion | flops 31457300 | bytes 4718612 | tf_op jit(solution)/shard_map/tk,kxz->txz/dot_general | solution.py:48
  274.0 2.8 slice_add_fusion
  277.7 32.9 %all-reduce.8.cloned.1.call-done = f32[512,256]{1,0:T(8,128)} async-done(((f32[512,256]{1,0:T(8,128)}), f32[512,256]{1,0:T(8,128)}) %all-reduce.8.cloned.1.call-update) | async-done | bytes 524304 | tf_op jit(solution)/shard_map/psum | solution.py:25
  310.7 1.7 fusion.24
  (33 shorter events, 9.8 us)
Async XLA Ops:
  6.5 51.5 %all-gather.4.cloned.1.call-start = ((), (), s32[]{:S(2)}) async-start(), calls=%async_computation | async-start | bytes 2359296 | tf_op jit(solution)/shard_map/all_gather | solution.py:33
  8.8 97.4 %all-reduce.4.cloned.1.call-start = ((), (), s32[]{:S(2)}) async-start(), calls=%async_computation.1 | async-start | bytes 1048576 | tf_op jit(solution)/shard_map/psum | solution.py:25
  73.2 83.7 %all-gather.6.cloned.1.call-start = ((), (), s32[]{:S(2)}) async-start(), calls=%async_computation.2 | async-start | bytes 2359296 | tf_op jit(solution)/shard_map/all_gather | solution.py:33
  108.5 101.0 %all-reduce.6.cloned.1.call-start = ((), (), s32[]{:S(2)}) async-start(), calls=%async_computation.3 | async-start | bytes 1048576 | tf_op jit(solution)/shard_map/psum | solution.py:25
  173.8 1.3 copy-start
  176.6 83.7 %all-gather.8.cloned.1.call-start = ((), (), s32[]{:S(2)}) async-start(), calls=%async_computation.4 | async-start | bytes 2359296 | tf_op jit(solution)/shard_map/all_gather | solution.py:33
  211.9 98.8 %all-reduce.8.cloned.1.call-start = ((), (), s32[]{:S(2)}) async-start(), calls=%async_computation.5 | async-start | bytes 1048576 | tf_op jit(solution)/shard_map/psum | solution.py:25
  276.9 35.5 %copy-start.1 = (bf16[512,256]{1,0:T(8,128)(2,1)S(1)}, bf16[512,256]{1,0:T(8,128)(2,1)}, u32[]{:S(2)}) copy-start(bf16[512,256]{1,0:T(8,128)(2,1)} %convolution_convert_fusion.3) | copy-start | bytes 786436
  276.9 35.5 %copy-start.2 = (bf16[256,512]{0,1:T(8,128)(2,1)S(1)}, bf16[256,512]{0,1:T(8,128)(2,1)}, u32[]{:S(2)}) copy-start(bf16[256,512]{0,1:T(8,128)(2,1)} %convolution_convert_fusion.2) | copy-start | bytes 786436
  276.9 35.5 %copy-start.3 = (bf16[256,512]{0,1:T(8,128)(2,1)S(1)}, bf16[256,512]{0,1:T(8,128)(2,1)}, u32[]{:S(2)}) copy-start(bf16[256,512]{0,1:T(8,128)(2,1)} %convolution_convert_fusion.1) | copy-start | bytes 786436
Sparse Core Ops, SparseCore 0:
  9.5 48.4 all-gather.3
  73.3 32.7 all-reduce.3
  108.6 48.1 all-gather.5
  176.7 32.7 all-reduce.5
  212.0 48.1 all-gather.7
  277.9 32.7 all-reduce.7
where the time goes:
time: 323 us; the launch traced here: 320 us
  waiting for transfers between devices  243 us (75%)
  matrix products  32.5 us (10%)
  local copies, waits for them, and re-layouts  26.2 us (8%)
  between operations  13.6 us (4%)
  other arithmetic  4.63 us (1%)
    all_gather x3, waiting for transfers between devices, on_device(): gathered = lax.all_gather(solved, 'prow', axis=0, tiled=True)  144 us
    psum x3, waiting for transfers between devices, on_device(): summed = lax.psum(partial_value[tree_level], 'pcol')  98.7 us
    dot_general x3, matrix products, on_device(): jnp.einsum('tk,kxz->txz', indicator_matrix, block_products, precision=lax...  12.8 us
    dot_general x3, local copies, waits for them, and re-layouts, on_device(): jnp.einsum('bij,bjr->bir', lower_blocks[0, 0, tree_level], picked, prefer...  12.1 us
    dot_general x3, matrix products, on_device(): jnp.einsum('bij,bjr->bir', lower_blocks[0, 0, tree_level], picked, prefer...  11 us
  transfers between devices with their start and end apart: 6, of which 6 were waited for; matrix products, arithmetic and copies ran while one was open for 0% of the time, Pallas kernels for 0%

commit v1 on v0

v1 whole, which is shorter than its diff:
```python
import functools

import jax
import jax.numpy as jnp
from jax import lax
from jax.experimental import pallas as pl
from jax.experimental.pallas import tpu as pltpu
from jax.sharding import PartitionSpec as P

MESH = pl.DeviceIdType.MESH
F32 = jnp.float32
BF16 = jnp.bfloat16


def kernel(dims, *refs):
    rows, cols, levels, width, half, slots = dims
    nx, ny = cols // 2, cols // 2
    nz = rows // nx
    per_col = rows // cols
    step_z = cols // nx
    (rhs_hbm, diag_hbm, low_hbm, src_ref, tgt_ref, out_hbm) = refs[:6]
    (rhs0, rhsh, diag, block, acc, mine, pair_out, pair_in, cross) = refs[6:15]
    low = refs[15:15 + levels - 1]
    (rhs_sem, diag_sem, low_sem, out_sem, b_send, b_recv, p_send, p_recv,
     y_send, y_recv, m_send, m_recv) = refs[15 + levels - 1:]

    r = lax.axis_index("prow")
    c = lax.axis_index("pcol")
    z, x = r // nx, lax.rem(r, nx)
    y, core = c // 2, lax.rem(c, 2)
    other = 1 - core
    spine_x = lax.rem(c, nx)
    is_spine = x == spine_x
    first_z = c // nx
    sibling = (r, y * 2 + other)

    def across(j):
        return (r, lax.rem(y + j, ny) * 2 + core)

    loads_rhs = [pltpu.make_async_copy(rhs_hbm.at[0, 0], rhs0, rhs_sem.at[0])]
    col_half = pl.ds(pl.multiple_of(core * half, half), half)
    for l in range(1, levels):
        loads_rhs.append(pltpu.make_async_copy(
            rhs_hbm.at[0, l, :, col_half], rhsh.at[l - 1], rhs_sem.at[l]))
    loads_diag = [pltpu.make_async_copy(diag_hbm.at[0, l], diag.at[l], diag_sem.at[l])
                  for l in range(levels)]
    loads_low = [pltpu.make_async_copy(
        low_hbm.at[0, 0, l, pl.ds(0, low[l].shape[0])], low[l], low_sem.at[l])
        for l in range(levels - 1)]
    for l in range(levels):
        loads_rhs[l].start()
        loads_diag[l].start()
        if l < levels - 1:
            loads_low[l].start()

    barrier = pltpu.get_barrier_semaphore()

    def greet(device):
        pl.semaphore_signal(barrier, inc=1, device_id=device, device_id_type=MESH)

    greet(sibling)
    for j in range(1, ny):
        greet(across(j))

    @pl.when(is_spine)
    def _():
        for j in range(1, nx):
            greet((z * nx + lax.rem(x + j, nx), c))

        @pl.when(z > 0)
        def _():
            greet((r - nx, c))

        @pl.when(z < nz - 1)
        def _():
            greet((r + nx, c))

    @pl.when(jnp.logical_not(is_spine))
    def _():
        greet((z * nx + spine_x, c))
    ends = jnp.where(z > 0, 1, 0) + jnp.where(z < nz - 1, 1, 0)
    pl.semaphore_wait(barrier, ny + jnp.where(is_spine, nx - 1 + ends, 1))

    def b_copy(l, k, h, lane, device):
        return pltpu.make_async_remote_copy(
            src_ref=block.at[l, k, h], dst_ref=block.at[l, k, h],
            send_sem=b_send.at[l, k, h, lane], recv_sem=b_recv.at[l, k, h],
            device_id=device, device_id_type=MESH)

    def on_routes(l, k, h, act):
        origin = first_z + k * step_z

        @pl.when(is_spine)
        def _():
            @pl.when(jnp.logical_and(z >= origin, z < nz - 1))
            def _():
                act(b_copy(l, k, h, 0, (r + nx, c)))

            @pl.when(jnp.logical_and(z <= origin, z > 0))
            def _():
                act(b_copy(l, k, h, 1, (r - nx, c)))
            for j in range(1, nx):
                act(b_copy(l, k, h, 1 + j, (z * nx + lax.rem(x + j, nx), c)))

    def is_root(k):
        return jnp.logical_and(is_spine, z == first_z + k * step_z)

    def publish(l, h, value):
        for k in range(per_col):
            @pl.when(is_root(k))
            def _():
                block[l, k, h] = value
                on_routes(l, k, h, lambda copy: copy.start())

    def p_copy(l):
        return pltpu.make_async_remote_copy(
            src_ref=pair_out.at[l], dst_ref=pair_in.at[l], send_sem=p_send.at[l],
            recv_sem=p_recv.at[l], device_id=sibling, device_id_type=MESH)

    def y_copy(l, j):
        return pltpu.make_async_remote_copy(
            src_ref=cross.at[l, y], dst_ref=cross.at[l, y], send_sem=y_send.at[l, j - 1],
            recv_sem=y_recv.at[l, j - 1], device_id=across(j), device_id_type=MESH)

    def m_copy(l):
        return pltpu.make_async_remote_copy(
            src_ref=mine.at[l, core], dst_ref=mine.at[l, core], send_sem=m_send.at[l],
            recv_sem=m_recv.at[l], device_id=sibling, device_id_type=MESH)

    def put_out(l):
        return [pltpu.make_async_copy(
            mine.at[l, h], out_hbm.at[0, l, :, pl.ds(h * half, half)], out_sem.at[l, h])
            for h in range(2)]

    def pair_slot(l, k, t):
        slot, there = jnp.int32(0), jnp.int32(0)
        for b in range(low[l].shape[0]):
            hit = jnp.where(
                jnp.logical_and(src_ref[0, 0, l, b] == k, tgt_ref[0, 0, l, b] == t), 1, 0)
            slot, there = slot + b * hit, there + hit
        return slot, there

    def product(l, k, t, right):
        slot, there = pair_slot(l, k, t)
        value = jnp.dot(low[l][slot], right, preferred_element_type=F32)
        if per_col * (levels - 1 - l) > slots:
            value = jnp.where(there > 0, value, 0.0)
        return value

    loads_rhs[0].wait()
    loads_diag[0].wait()
    solved = jnp.dot(diag[0], rhs0[...].astype(BF16), preferred_element_type=F32).astype(BF16)
    for h in range(2):
        publish(0, h, solved[:, h * half:(h + 1) * half])
    for h in range(2):
        mine[0, h] = solved[:, h * half:(h + 1) * half]
    for copy in put_out(0):
        copy.start()

    low_z = z < nz // 2
    for l in range(levels - 1):
        t = l + 1
        for i in range(per_col):
            k = jnp.where(low_z, i, per_col - 1 - i)
            for h in (core, other):
                @pl.when(jnp.logical_not(is_root(k)))
                def _():
                    b_copy(l, k, h, 0, sibling).wait_recv()
                    on_routes(l, k, h, lambda copy: copy.start())
        loads_low[l].wait()

        def next_partial(h):
            total = None
            for k in range(per_col):
                value = product(l, k, t, block[l, k, h])
                total = value if total is None else total + value
            if l > 0:
                total = total + acc[t - 1, h]
            return total

        pair_out[l] = next_partial(other).astype(BF16)
        p_copy(l).start()
        own = next_partial(core)
        p_copy(l).wait_recv()
        cross[l, y] = (own + pair_in[l].astype(F32)).astype(BF16)
        for j in range(1, ny):
            y_copy(l, j).start()

        for later in range(l + 2, levels):
            total = None
            for k in range(per_col):
                right = jnp.concatenate([block[l, k, 0], block[l, k, 1]], axis=1)
                value = product(l, k, later, right)
                total = value if total is None else total + value
            for h in range(2):
                part = total[:, h * half:(h + 1) * half]
                acc[later - 1, h] = part if l == 0 else acc[later - 1, h] + part

        loads_rhs[t].wait()
        loads_diag[t].wait()
        for j in range(1, ny):
            y_copy(l, j).wait_recv()
        summed = cross[l, 0].astype(F32)
        for j in range(1, ny):
            summed = summed + cross[l, j].astype(F32)
        reduced = (rhsh[t - 1] - summed).astype(BF16)
        solved = jnp.dot(diag[t], reduced, preferred_element_type=F32).astype(BF16)
        mine[t, core] = solved
        m_copy(t).start()
        if t < levels - 1:
            publish(t, core, solved)
        m_copy(t).wait_recv()
        if t < levels - 1:
            publish(t, other, mine[t, other])
        for copy in put_out(t):
            copy.start()

    for l in range(levels):
        for copy in put_out(l):
            copy.wait()
        if l > 0:
            m_copy(l).wait_send()
        if l < levels - 1:
            p_copy(l).wait_send()
            for j in range(1, ny):
                y_copy(l, j).wait_send()
            for k in range(per_col):
                for h in range(2):
                    on_routes(l, k, h, lambda copy: copy.wait_send())


def on_device(mesh_sizes, right_hand_blocks, diag_inverse, lower_blocks, block_source,
              target_level_per_slot):
    rows, cols = mesh_sizes
    _, levels, width, rhs_cols = right_hand_blocks.shape
    slots = lower_blocks.shape[3]
    half = rhs_cols // 2
    per_col = rows // cols
    nx, ny = cols // 2, cols // 2
    filled = [min(slots, per_col * (levels - 1 - l)) for l in range(levels - 1)]
    dma = pltpu.SemaphoreType.DMA
    steps = levels - 1
    piece = (width, half)
    products = sum(filled) + levels
    return pl.pallas_call(
        functools.partial(kernel, (rows, cols, levels, width, half, slots)),
        out_shape=jax.ShapeDtypeStruct((1, levels, width, rhs_cols), BF16),
        in_specs=[pl.BlockSpec(memory_space=pl.ANY)] * 3
        + [pl.BlockSpec(memory_space=pltpu.SMEM)] * 2,
        out_specs=pl.BlockSpec(memory_space=pl.ANY),
        scratch_shapes=[
            pltpu.VMEM((width, rhs_cols), F32),
            pltpu.VMEM((steps,) + piece, F32),
            pltpu.VMEM((levels, width, width), BF16),
            pltpu.VMEM((steps, per_col, 2) + piece, BF16),
            pltpu.VMEM((steps, 2) + piece, F32),
            pltpu.VMEM((levels, 2) + piece, BF16),
            pltpu.VMEM((steps,) + piece, BF16),
            pltpu.VMEM((steps,) + piece, BF16),
            pltpu.VMEM((steps, ny) + piece, BF16),
        ]
        + [pltpu.VMEM((n, width, width), BF16) for n in filled]
        + [
            dma((levels,)), dma((levels,)), dma((steps,)), dma((levels, 2)),
            dma((steps, per_col, 2, nx + 1)), dma((steps, per_col, 2)),
            dma((steps,)), dma((steps,)),
            dma((steps, ny - 1)), dma((steps, ny - 1)),
            dma((levels,)), dma((levels,)),
        ],
        compiler_params=pltpu.CompilerParams(
            collective_id=0, has_side_effects=True, vmem_limit_bytes=56 * 2**20),
        cost_estimate=pl.CostEstimate(
            flops=2 * products * width * width * rhs_cols,
            bytes_accessed=products * width * width * 2 + levels * width * rhs_cols * 6,
            transcendentals=0),
    )(right_hand_blocks, diag_inverse, lower_blocks, block_source, target_level_per_slot)


def solution(mesh):
    placed = (
        P("prow", None, None, None),
        P("prow", None, None, None),
        P("prow", "pcol", None, None, None, None),
        P("prow", "pcol", None, None),
        P("prow", "pcol", None, None),
    )
    sizes = (mesh.shape["prow"], mesh.shape["pcol"])
    return jax.shard_map(
        functools.partial(on_device, sizes),
        mesh=mesh,
        in_specs=placed,
        out_specs=P("prow", None, None, None),
        check_vma=False,
    )
```

time: 323 us -> 80 us (0.25)
  waiting for transfers between devices: 243 us -> 0 us
  Pallas kernels: 0 us -> 75 us
  matrix products: 32.5 us -> 0 us
  local copies, waits for them, and re-layouts: 26.2 us -> 4.79 us
  between operations: 13.6 us -> 0.01 us
  other arithmetic: 4.63 us -> 0 us
    all_gather x3 -> x0, waiting for transfers between devices: 144 us -> none  [on_device(): gathered = lax.all_gather(solved, 'prow', axis=0, tiled=True)]
    psum x3 -> x0, waiting for transfers between devices: 98.7 us -> none  [on_device(): summed = lax.psum(partial_value[tree_level], 'pcol')]
    pallas_call x0 -> x1, Pallas kernels: none -> 75 us  [on_device(): pl.pallas_call(functools.partial(kernel, (rows, cols, levels, width, half...]
    dot_general x10 -> x0, matrix products: 32.5 us -> none  [the longest x3 12.8 us: on_device(): jnp.einsum('tk,kxz->txz', indicator_matrix, block_products, precision=lax...]
    dot_general x3 -> x0, local copies, waits for them, and re-layouts: 12.1 us -> none  [on_device(): jnp.einsum('bij,bjr->bir', lower_blocks[0, 0, tree_level], picked, prefer...]
    gather x3 -> x0, local copies, waits for them, and re-layouts: 5.34 us -> none  [on_device(): picked = jnp.take(by_slot, sources, axis=0)]
  transfers between devices with their start and end apart: 6 -> 0, of which waited for: 6 -> 0; matrix products, arithmetic and copies ran while one was open for 0% -> 0% of each run, Pallas kernels for 0% -> 0%
where the time goes in v1:
time: 80 us; the launch traced here: 79.8 us
  Pallas kernels  75 us (94%)
  local copies, waits for them, and re-layouts  4.79 us (6%)
    pallas_call x1, Pallas kernels, on_device(): pl.pallas_call(functools.partial(kernel, (rows, cols, levels, width, half...  75 us
    unnamed x3, local copies, waits for them, and re-layouts  4.79 us

profile of v1, /device:TPU:3, one launch (start us, length us, event | category | flops | bytes accessed | tf_op | source)
XLA Modules:
  0.0 79.8 jit_solution(896880995248315029)
XLA Ops:
  0.0 1.3 %copy.6.refs_3_ = s32[1,1,3,5]{3,2,1,0:T(4,128)} copy(s32[1,1,3,5]{3,1,2,0:T(1,128)} %param.8) | data formatting | bytes 120 | tf_op args[3]
  1.3 1.3 %copy.7.refs_4_ = s32[1,1,3,5]{3,2,1,0:T(4,128)} copy(s32[1,1,3,5]{3,1,2,0:T(1,128)} %param.9) | data formatting | bytes 120 | tf_op args[4]
  2.5 75.0 %shard_map.55 = bf16[1,4,512,256]{3,2,1,0:T(8,128)(2,1)} custom-call(f32[1,4,512,256]{3,2,1,0:T(8,128)} %refs_0_.1, bf16[1,4,512,512]{3,2,1,0:T(8,128)(2,1)} %refs_1_.1, bf16[1,1,3,5,512,512]{5,4,3,2,1,0:T(8,128)(2,1)} %refs_2_.1, s32[1,1,3,5]{3,2,1,0:T(4,128)} %copy.6.refs_3_, s32[1,1,3,5]{3,2,1,0:T(4,128)} %copy.7.refs_4_), custom_call_target="tpu_custom_call" | custom-call | flops 2013265920 | bytes 11010048 | tf_op jit(solution)/shard_map/pallas_call | solution.py:245
  77.6 2.3 %copy.9 = bf16[1,4,512,256]{3,2,1,0:T(8,128)(2,1)} copy(bf16[1,4,512,256]{3,2,1,0:T(8,128)(2,1)} %shard_map.55) | data formatting | bytes 2097152

commit v2 on v1

--- a/solution.py
+++ b/solution.py
@@ -10,6 +10,7 @@
 MESH = pl.DeviceIdType.MESH
 F32 = jnp.float32
 BF16 = jnp.bfloat16
+PIECES = 4
 
 
 def kernel(dims, *refs):
@@ -18,11 +19,11 @@
     nz = rows // nx
     per_col = rows // cols
     step_z = cols // nx
-    (rhs_hbm, diag_hbm, low_hbm, src_ref, tgt_ref, out_hbm) = refs[:6]
+    (rhs_hbm, diag_hbm, low_hbm, src_hbm, tgt_hbm, out_hbm) = refs[:6]
     (rhs0, rhsh, diag, block, acc, mine, pair_out, pair_in, cross) = refs[6:15]
     low = refs[15:15 + levels - 1]
     (rhs_sem, diag_sem, low_sem, out_sem, b_send, b_recv, p_send, p_recv,
-     y_send, y_recv, m_send, m_recv) = refs[15 + levels - 1:]
+     y_send, y_recv, m_send, m_recv, src_ref, tgt_ref, table_sem) = refs[15 + levels - 1:]
 
     r = lax.axis_index("prow")
     c = lax.axis_index("pcol")
@@ -53,6 +54,11 @@
         if l < levels - 1:
             loads_low[l].start()
 
+    tables = [pltpu.make_async_copy(src_hbm, src_ref, table_sem.at[0]),
+              pltpu.make_async_copy(tgt_hbm, tgt_ref, table_sem.at[1])]
+    for copy in tables:
+        copy.start()
+
     barrier = pltpu.get_barrier_semaphore()
 
     def greet(device):
@@ -81,26 +87,29 @@
     ends = jnp.where(z > 0, 1, 0) + jnp.where(z < nz - 1, 1, 0)
     pl.semaphore_wait(barrier, ny + jnp.where(is_spine, nx - 1 + ends, 1))
 
-    def b_copy(l, k, h, lane, device):
+    piece_rows = width // PIECES
+
+    def b_copy(l, k, h, p, lane, device):
+        part = block.at[l, k, h, pl.ds(p * piece_rows, piece_rows)]
         return pltpu.make_async_remote_copy(
-            src_ref=block.at[l, k, h], dst_ref=block.at[l, k, h],
-            send_sem=b_send.at[l, k, h, lane], recv_sem=b_recv.at[l, k, h],
+            src_ref=part, dst_ref=part,
+            send_sem=b_send.at[l, k, h, p, lane], recv_sem=b_recv.at[l, k, h, p],
             device_id=device, device_id_type=MESH)
 
-    def on_routes(l, k, h, act):
+    def on_routes(l, k, h, p, act):
         origin = first_z + k * step_z
 
         @pl.when(is_spine)
         def _():
             @pl.when(jnp.logical_and(z >= origin, z < nz - 1))
             def _():
-                act(b_copy(l, k, h, 0, (r + nx, c)))
+                act(b_copy(l, k, h, p, 0, (r + nx, c)))
 
             @pl.when(jnp.logical_and(z <= origin, z > 0))
             def _():
-                act(b_copy(l, k, h, 1, (r - nx, c)))
+                act(b_copy(l, k, h, p, 1, (r - nx, c)))
             for j in range(1, nx):
-                act(b_copy(l, k, h, 1 + j, (z * nx + lax.rem(x + j, nx), c)))
+                act(b_copy(l, k, h, p, 1 + j, (z * nx + lax.rem(x + j, nx), c)))
 
     def is_root(k):
         return jnp.logical_and(is_spine, z == first_z + k * step_z)
@@ -110,7 +119,8 @@
             @pl.when(is_root(k))
             def _():
                 block[l, k, h] = value
-                on_routes(l, k, h, lambda copy: copy.start())
+                for p in range(PIECES):
+                    on_routes(l, k, h, p, lambda copy: copy.start())
 
     def p_copy(l):
         return pltpu.make_async_remote_copy(
@@ -157,6 +167,8 @@
     for copy in put_out(0):
         copy.start()
 
+    for copy in tables:
+        copy.wait()
     low_z = z < nz // 2
     for l in range(levels - 1):
         t = l + 1
@@ -165,8 +177,9 @@
             for h in (core, other):
                 @pl.when(jnp.logical_not(is_root(k)))
                 def _():
-                    b_copy(l, k, h, 0, sibling).wait_recv()
-                    on_routes(l, k, h, lambda copy: copy.start())
+                    for p in range(PIECES):
+                        b_copy(l, k, h, p, 0, sibling).wait_recv()
+                        on_routes(l, k, h, p, lambda copy: copy.start())
         loads_low[l].wait()
 
         def next_partial(h):
@@ -226,7 +239,8 @@
                 y_copy(l, j).wait_send()
             for k in range(per_col):
                 for h in range(2):
-                    on_routes(l, k, h, lambda copy: copy.wait_send())
+                    for p in range(PIECES):
+                        on_routes(l, k, h, p, lambda copy: copy.wait_send())
 
 
 def on_device(mesh_sizes, right_hand_blocks, diag_inverse, lower_blocks, block_source,
@@ -245,8 +259,7 @@
     return pl.pallas_call(
         functools.partial(kernel, (rows, cols, levels, width, half, slots)),
         out_shape=jax.ShapeDtypeStruct((1, levels, width, rhs_cols), BF16),
-        in_specs=[pl.BlockSpec(memory_space=pl.ANY)] * 3
-        + [pl.BlockSpec(memory_space=pltpu.SMEM)] * 2,
+        in_specs=[pl.BlockSpec(memory_space=pl.ANY)] * 5,
         out_specs=pl.BlockSpec(memory_space=pl.ANY),
         scratch_shapes=[
             pltpu.VMEM((width, rhs_cols), F32),
@@ -262,10 +275,12 @@
         + [pltpu.VMEM((n, width, width), BF16) for n in filled]
         + [
             dma((levels,)), dma((levels,)), dma((steps,)), dma((levels, 2)),
-            dma((steps, per_col, 2, nx + 1)), dma((steps, per_col, 2)),
+            dma((steps, per_col, 2, PIECES, nx + 1)), dma((steps, per_col, 2, PIECES)),
             dma((steps,)), dma((steps,)),
             dma((steps, ny - 1)), dma((steps, ny - 1)),
             dma((levels,)), dma((levels,)),
+            pltpu.SMEM(block_source.shape, jnp.int32),
+            pltpu.SMEM(target_level_per_slot.shape, jnp.int32), dma((2,)),
         ],
         compiler_params=pltpu.CompilerParams(
             collective_id=0, has_side_effects=True, vmem_limit_bytes=56 * 2**20),

time: 80 us -> 71.7 us (0.90)
  Pallas kernels: 75 us -> 66.7 us
    pallas_call x1, Pallas kernels: 75 us -> 66.7 us  [on_device(): pl.pallas_call(functools.partial(kernel, (rows, cols, levels, width, half...]
where the time goes in v2:
time: 71.7 us; the launch traced here: 71.5 us
  Pallas kernels  66.7 us (93%)
  local copies, waits for them, and re-layouts  4.79 us (7%)
    pallas_call x1, Pallas kernels, on_device(): pl.pallas_call(functools.partial(kernel, (rows, cols, levels, width, half...  66.7 us
    unnamed x3, local copies, waits for them, and re-layouts  4.79 us

profile of v2, /device:TPU:3, one launch (start us, length us, event | category | flops | bytes accessed | tf_op | source)
XLA Modules:
  0.0 71.5 jit_solution(12353665954050401738)
XLA Ops:
  0.0 1.3 %copy.6.refs_3_ = s32[1,1,3,5]{3,2,1,0:T(4,128)} copy(s32[1,1,3,5]{3,1,2,0:T(1,128)} %param.8) | data formatting | bytes 120 | tf_op args[3]
  1.3 1.3 %copy.7.refs_4_ = s32[1,1,3,5]{3,2,1,0:T(4,128)} copy(s32[1,1,3,5]{3,1,2,0:T(1,128)} %param.9) | data formatting | bytes 120 | tf_op args[4]
  2.5 66.7 %shard_map.55 = bf16[1,4,512,256]{3,2,1,0:T(8,128)(2,1)} custom-call(f32[1,4,512,256]{3,2,1,0:T(8,128)} %refs_0_.1, bf16[1,4,512,512]{3,2,1,0:T(8,128)(2,1)} %refs_1_.1, bf16[1,1,3,5,512,512]{5,4,3,2,1,0:T(8,128)(2,1)} %refs_2_.1, s32[1,1,3,5]{3,2,1,0:T(4,128)} %copy.6.refs_3_, s32[1,1,3,5]{3,2,1,0:T(4,128)} %copy.7.refs_4_), custom_call_target="tpu_custom_call" | custom-call | flops 2013265920 | bytes 11010048 | tf_op jit(solution)/shard_map/pallas_call | solution.py:259
  69.2 2.3 %copy.9 = bf16[1,4,512,256]{3,2,1,0:T(8,128)(2,1)} copy(bf16[1,4,512,256]{3,2,1,0:T(8,128)(2,1)} %shard_map.55) | data formatting | bytes 2097152

commit v3 on v2

--- a/solution.py
+++ b/solution.py
@@ -85,7 +85,6 @@
     def _():
         greet((z * nx + spine_x, c))
     ends = jnp.where(z > 0, 1, 0) + jnp.where(z < nz - 1, 1, 0)
-    pl.semaphore_wait(barrier, ny + jnp.where(is_spine, nx - 1 + ends, 1))
 
     piece_rows = width // PIECES
 
@@ -160,6 +159,7 @@
     loads_rhs[0].wait()
     loads_diag[0].wait()
     solved = jnp.dot(diag[0], rhs0[...].astype(BF16), preferred_element_type=F32).astype(BF16)
+    pl.semaphore_wait(barrier, ny + jnp.where(is_spine, nx - 1 + ends, 1))
     for h in range(2):
         publish(0, h, solved[:, h * half:(h + 1) * half])
     for h in range(2):

time: 71.7 us -> 71.4 us (level)
  no operation moved by 1% of the time
where the time goes in v3:
time: 71.4 us; the launch traced here: 71.2 us
  Pallas kernels  66.4 us (93%)
  local copies, waits for them, and re-layouts  4.79 us (7%)
    pallas_call x1, Pallas kernels, on_device(): pl.pallas_call(functools.partial(kernel, (rows, cols, levels, width, half...  66.4 us
    unnamed x3, local copies, waits for them, and re-layouts  4.79 us

profile of v3, /device:TPU:3, one launch (start us, length us, event | category | flops | bytes accessed | tf_op | source)
XLA Modules:
  0.0 71.2 jit_solution(4813749819243603195)
XLA Ops:
  0.0 1.3 %copy.6.refs_3_ = s32[1,1,3,5]{3,2,1,0:T(4,128)} copy(s32[1,1,3,5]{3,1,2,0:T(1,128)} %param.8) | data formatting | bytes 120 | tf_op args[3]
  1.3 1.3 %copy.7.refs_4_ = s32[1,1,3,5]{3,2,1,0:T(4,128)} copy(s32[1,1,3,5]{3,1,2,0:T(1,128)} %param.9) | data formatting | bytes 120 | tf_op args[4]
  2.5 66.4 %shard_map.55 = bf16[1,4,512,256]{3,2,1,0:T(8,128)(2,1)} custom-call(f32[1,4,512,256]{3,2,1,0:T(8,128)} %refs_0_.1, bf16[1,4,512,512]{3,2,1,0:T(8,128)(2,1)} %refs_1_.1, bf16[1,1,3,5,512,512]{5,4,3,2,1,0:T(8,128)(2,1)} %refs_2_.1, s32[1,1,3,5]{3,2,1,0:T(4,128)} %copy.6.refs_3_, s32[1,1,3,5]{3,2,1,0:T(4,128)} %copy.7.refs_4_), custom_call_target="tpu_custom_call" | custom-call | flops 2013265920 | bytes 11010048 | tf_op jit(solution)/shard_map/pallas_call | solution.py:259
  68.9 2.3 %copy.9 = bf16[1,4,512,256]{3,2,1,0:T(8,128)(2,1)} copy(bf16[1,4,512,256]{3,2,1,0:T(8,128)(2,1)} %shard_map.55) | data formatting | bytes 2097152
